TPU v7x, 32 devices: a whole 2x2x4 slice. The times are simulated.
32 devices in a mesh: row: 4 (over y, x), col: 8 (over z, core).
Axes of the slice: x: 2, y: 2, z: 4, core: 2. Of those that a mesh axis runs over, the one named last changes fastest.
Arguments:
- galaxy: float32 [128, 256, 256], P('row', 'col'), may hold values from 0.03 to 32, as said below
- randoms: float32 [128, 256, 256], P('row', 'col'), may hold values from 0.5 to 4
- coverage: int32 [128, 256, 256], P('row', 'col'), may hold values from 0 to 1
- patch: int32 [128, 256, 256], P('row', 'col'), may hold values from 0 to 127
Outputs:
- contrast: float32 [128, 256, 256], P('row', 'col')
- patch_sums: float32 [4, 128], replicated
Inputs may be any that keep to these rules, and one draw needn't show every extreme that they name: `galaxy`: positive densities.
All inputs are finite; a program needn't handle non-finite values.
Results may differ from a plain program's by a relative error of at most 0.00016.
Values sent between devices are 32-bit elements; how exact they have to be, the bound alone decides.
A program may use at most 64 MiB of HBM per device.

v0:
```python
import jax
import jax.numpy as jnp
from jax import lax
from jax.sharding import PartitionSpec as P

RADIUS = 16
NPATCH = 128


def extended_2(array, sides, width):
    for axis, dim in sides:
        devices, length = (lax.axis_size(axis), array.shape[dim])
        up = [(i, (i + 1) % devices) for i in range(devices - 1)]
        down = [(j, i) for i, j in up]
        last = lax.slice_in_dim(array, length - width, length, axis=dim)
        first = lax.slice_in_dim(array, 0, width, axis=dim)
        before = lax.ppermute(last, axis, up)
        after = lax.ppermute(first, axis, down)
        array = jnp.concatenate([before, array, after], axis=dim)
    return array


def kernel_taps(radius):
    offs = jnp.arange(-radius, radius + 1).astype(jnp.float32)
    sigma = radius / 2.0
    vals = jnp.exp(-offs * offs / (2.0 * sigma * sigma))
    return vals / jnp.sum(vals)


def valid_taps(padded, taps, radius, axis):
    count = padded.shape[axis] - 2 * radius
    total = lax.slice_in_dim(padded, 0, count, axis=axis) * taps[0]
    for j in range(1, 2 * radius + 1):
        total = total + taps[j] * lax.slice_in_dim(padded, j, j + count, axis=axis)
    return total


def local(galaxy, randoms, coverage, patch):
    radius = RADIUS
    taps = kernel_taps(radius)
    fields = jnp.stack([galaxy, randoms])
    widths = ((0, 0), (0, 0), (0, 0), (radius, radius))
    zsmooth = valid_taps(jnp.pad(fields, widths), taps, radius, 3)
    cover = coverage.astype(jnp.float32)
    totals = lax.psum((jnp.sum(cover * galaxy), jnp.sum(cover * randoms)), ("row", "col"))
    extended = extended_2(zsmooth, (("row", 1), ("col", 2)), radius)
    xsmooth = valid_taps(extended, taps, radius, 1)
    smoothed = valid_taps(xsmooth, taps, radius, 2)
    alpha = totals[0] / totals[1]
    nbar = alpha * smoothed[1]
    weight = 1.0 / (1.0 + 2.0 * nbar)
    contrast = cover * weight * (smoothed[0] / nbar - 1.0)
    rows_x, rows_y, depth = contrast.shape
    per_row = rows_y * depth
    block = 1
    for cand in range(1, rows_x + 1):
        if rows_x % cand == 0 and cand * per_row <= 32768:
            block = cand
    steps_count = rows_x // block
    flat_c = contrast.reshape(steps_count, block * per_row)
    flat_m = cover.reshape(steps_count, block * per_row)
    flat_p = patch.reshape(steps_count, block * per_row)
    labels = jnp.arange(NPATCH, dtype=jnp.int32)

    def accumulate(carry, items):
        cvals, mvals, pvals = items
        powers = jnp.stack(
            [mvals, mvals * cvals, mvals * cvals * cvals, mvals * cvals * cvals * cvals]
        )
        onehot = (pvals[None, :] == labels[:, None]).astype(jnp.float32)
        part_sums = lax.dot_general(
            powers,
            onehot,
            (((1,), (1,)), ((), ())),
            precision=lax.Precision.HIGHEST,
            preferred_element_type=jnp.float32,
        )
        return (carry + part_sums, None)

    local_sums, unused = lax.scan(
        accumulate, jnp.zeros((4, NPATCH), jnp.float32), (flat_c, flat_m, flat_p)
    )
    whole_sums = lax.psum(local_sums, ("row", "col"))
    scale = NPATCH / (rows_x * lax.axis_size("row") * rows_y * lax.axis_size("col") * depth)
    return (contrast, whole_sums * scale)


def solution(mesh):
    in_specs = (
        P("row", "col", None),
        P("row", "col", None),
        P("row", "col", None),
        P("row", "col", None),
    )
    out_specs = (P("row", "col", None), P())
    return jax.shard_map(local, mesh=mesh, in_specs=in_specs, out_specs=out_specs, check_vma=False)
```

profile of v0, /device:TPU:0, one launch (start us, length us, event | category | flops | bytes accessed | tf_op | source)
XLA Modules:
  0.0 384.6 jit_solution(8935265958357768094)
XLA Ops:
  3.4 3.1 pad_maximum_fusion.2
  6.5 64.2 %fusion.99 = f32[2,32,32,256]{3,2,1,0:T(8,128)S(1)} fusion(f32[2,32,32,256]{3,2,1,0:T(8,128)} %pad_maximum_fusion.2, f32[]{:T(128)} %bitcast.34, f32[]{:T(128)} %bitcast.33, f32[]{:T(128)} %bitcast.32, f32[]{:T(128)} %bitcast.31, f32[]{:T(128)} %bitcast.30, f32[]{:T(128)} %bitcast.29, f32[]{:T(128)} %bitcast.28, f32[]{:T(128)} %bitcast.27, f32[]{:T(128)} %bitcast.26, ...), kind=kLoop, calls=%fused_computation.171 | loop fusion | flops 34078720 | bytes 4194436 | tf_op jit(solution)/shard_map/add | solution.py:34
  70.9 4.9 %collective-permute-start = (f32[2,16,32,256]{3,2,1,0:T(8,128)S(1)}, f32[2,16,32,256]{3,2,1,0:T(8,128)S(1)}, u32[]{:S(2)}, u32[]{:S(2)}) collective-permute-start(f32[2,16,32,256]{3,2,1,0:T(8,128)S(1)} %get-tuple-element.75), channel_id=1, source_target_pairs={{0,8},{8,16},{16,24},{1,9},{9,17},{17,25},{2,10},{10,18},{18,26},{... | collective-permute-start | bytes 3145736 | tf_op jit(solution)/shard_map/ppermute | solution.py:17
  77.2 21.0 %collective-permute-done = f32[2,16,32,256]{3,2,1,0:T(8,128)S(1)} collective-permute-done((f32[2,16,32,256]{3,2,1,0:T(8,128)S(1)}, f32[2,16,32,256]{3,2,1,0:T(8,128)S(1)}, u32[]{:S(2)}, u32[]{:S(2)}) %collective-permute-start) | collective-permute-done | bytes 1048608 | tf_op jit(solution)/shard_map/ppermute | solution.py:17
  98.2 24.4 %collective-permute-done.1 = f32[2,16,32,256]{3,2,1,0:T(8,128)S(1)} collective-permute-done((f32[2,16,32,256]{3,2,1,0:T(8,128)S(1)}, f32[2,16,32,256]{3,2,1,0:T(8,128)S(1)}, u32[]{:S(2)}, u32[]{:S(2)}) %collective-permute-start.1) | collective-permute-done | bytes 1048608 | tf_op jit(solution)/shard_map/ppermute | solution.py:18
  123.7 2.4 fusion.147
  126.1 2.6 collective-permute-start.2
  131.1 46.6 %all-reduce.1 = (f32[]{:T(128)}, f32[]{:T(128)}) all-reduce(f32[]{:T(128)} %get-tuple-element.56, f32[]{:T(128)} %get-tuple-element.55), channel_id=1, replica_groups=mesh['row'=4,'col'=8] {'row','col'}, use_global_device_ids=true, to_apply=%region_1.2 | all-reduce | flops 2 | bytes 16 | tf_op jit(solution)/shard_map/psum | solution.py:45
  178.8 2.5 reshape.25
  181.3 2.4 reshape.27
  185.0 3.3 pad_maximum_fusion
  188.3 36.4 %fusion.13 = f32[2,32,64,256]{3,2,1,0:T(8,128)S(1)} fusion(f32[2,64,64,256]{3,2,1,0:T(8,128)S(1)} %pad_maximum_fusion, f32[]{:T(128)} %bitcast.34, f32[]{:T(128)} %bitcast.33, f32[]{:T(128)} %bitcast.32, f32[]{:T(128)} %bitcast.31, f32[]{:T(128)} %bitcast.30, f32[]{:T(128)} %bitcast.29, f32[]{:T(128)} %bitcast.28, f32[]{:T(128)} %bitcast.27, f32[]{:T(128)} %bitcast.26, ...), kind=kLoop, calls=%fused_computation.52 | loop fusion | flops 68157440 | bytes 142606464 | tf_op jit(solution)/shard_map/add | solution.py:34
  224.8 28.9 %fusion.109 = f32[2,32,32,256]{3,2,1,0:T(8,128)S(1)} fusion(f32[2,32,64,256]{3,2,1,0:T(8,128)S(1)} %fusion.13, f32[]{:T(128)} %bitcast.34, f32[]{:T(128)} %bitcast.33, f32[]{:T(128)} %bitcast.32, f32[]{:T(128)} %bitcast.31, f32[]{:T(128)} %bitcast.30, f32[]{:T(128)} %bitcast.29, f32[]{:T(128)} %bitcast.28, f32[]{:T(128)} %bitcast.27, f32[]{:T(128)} %bitcast.26, ...), kind=kLoop, calls=%fused_computation.182 | loop fusion | flops 34078720 | bytes 71303296 | tf_op jit(solution)/shard_map/add | solution.py:34
  255.0 87.6 %while.11 = (s32[]{:T(128)}, f32[4,128]{1,0:T(4,128)S(1)}, f32[8,32768]{1,0:T(8,128)}, f32[8,32768]{1,0:T(8,128)S(1)}, s32[8,32768]{1,0:T(8,128)}, /*index=5*/s32[]{:T(128)}, s32[]{:T(128)}) while((s32[]{:T(128)}, f32[4,128]{1,0:T(4,128)S(1)}, f32[8,32768]{1,0:T(8,128)}, f32[8,32768]{1,0:T(8,128)S(1)}, s32[8,32768]{1,0:T(8,128)}, ...), condition=%wide.region_6.7_spmd.clone, body=%wide.region_5.6_spmd.clone.sunk | while | flops 206013440 | bytes 1708127 | solution.py:80
  257.8 8.1 %fusion.154 = f32[4,128]{1,0:T(4,128)S(1)} fusion(s32[32768]{0:T(1024)S(1)} %bitcast.48, f32[1,32768]{1,0:T(1,128)S(1)} %get-tuple-element.145, f32[1,32768]{1,0:T(1,128)S(1)} %get-tuple-element.146, f32[1,32768]{1,0:T(1,128)S(1)} %get-tuple-element.147, f32[1,32768]{1,0:T(1,128)S(1)} %get-tuple-element.148, f32[4,128]{1,0:T(4,128)S(1)} %get-tuple-element.157, ...), kind=kOutput, calls=%fused_computation.4.clone.1 | convolution fusion | flops 205915136 | bytes 659457 | tf_op jit(solution)/shard_map/while/body/eval_jaxpr/dot_general | solution.py:71
  265.9 1.5 dynamic-slice_multiply_fusion.6
  268.8 8.1 %fusion.154 = f32[4,128]{1,0:T(4,128)S(1)} fusion(s32[32768]{0:T(1024)S(1)} %bitcast.48, f32[1,32768]{1,0:T(1,128)S(1)} %get-tuple-element.145, f32[1,32768]{1,0:T(1,128)S(1)} %get-tuple-element.146, f32[1,32768]{1,0:T(1,128)S(1)} %get-tuple-element.147, f32[1,32768]{1,0:T(1,128)S(1)} %get-tuple-element.148, f32[4,128]{1,0:T(4,128)S(1)} %get-tuple-element.157, ...), kind=kOutput, calls=%fused_computation.4.clone.1 | convolution fusion | flops 205915136 | bytes 659457 | tf_op jit(solution)/shard_map/while/body/eval_jaxpr/dot_general | solution.py:71
  279.7 8.1 %fusion.154 = f32[4,128]{1,0:T(4,128)S(1)} fusion(s32[32768]{0:T(1024)S(1)} %bitcast.48, f32[1,32768]{1,0:T(1,128)S(1)} %get-tuple-element.145, f32[1,32768]{1,0:T(1,128)S(1)} %get-tuple-element.146, f32[1,32768]{1,0:T(1,128)S(1)} %get-tuple-element.147, f32[1,32768]{1,0:T(1,128)S(1)} %get-tuple-element.148, f32[4,128]{1,0:T(4,128)S(1)} %get-tuple-element.157, ...), kind=kOutput, calls=%fused_computation.4.clone.1 | convolution fusion | flops 205915136 | bytes 659457 | tf_op jit(solution)/shard_map/while/body/eval_jaxpr/dot_general | solution.py:71
  290.7 8.1 %fusion.154 = f32[4,128]{1,0:T(4,128)S(1)} fusion(s32[32768]{0:T(1024)S(1)} %bitcast.48, f32[1,32768]{1,0:T(1,128)S(1)} %get-tuple-element.145, f32[1,32768]{1,0:T(1,128)S(1)} %get-tuple-element.146, f32[1,32768]{1,0:T(1,128)S(1)} %get-tuple-element.147, f32[1,32768]{1,0:T(1,128)S(1)} %get-tuple-element.148, f32[4,128]{1,0:T(4,128)S(1)} %get-tuple-element.157, ...), kind=kOutput, calls=%fused_computation.4.clone.1 | convolution fusion | flops 205915136 | bytes 659457 | tf_op jit(solution)/shard_map/while/body/eval_jaxpr/dot_general | solution.py:71
  301.7 8.1 %fusion.154 = f32[4,128]{1,0:T(4,128)S(1)} fusion(s32[32768]{0:T(1024)S(1)} %bitcast.48, f32[1,32768]{1,0:T(1,128)S(1)} %get-tuple-element.145, f32[1,32768]{1,0:T(1,128)S(1)} %get-tuple-element.146, f32[1,32768]{1,0:T(1,128)S(1)} %get-tuple-element.147, f32[1,32768]{1,0:T(1,128)S(1)} %get-tuple-element.148, f32[4,128]{1,0:T(4,128)S(1)} %get-tuple-element.157, ...), kind=kOutput, calls=%fused_computation.4.clone.1 | convolution fusion | flops 205915136 | bytes 659457 | tf_op jit(solution)/shard_map/while/body/eval_jaxpr/dot_general | solution.py:71
  312.6 8.1 %fusion.154 = f32[4,128]{1,0:T(4,128)S(1)} fusion(s32[32768]{0:T(1024)S(1)} %bitcast.48, f32[1,32768]{1,0:T(1,128)S(1)} %get-tuple-element.145, f32[1,32768]{1,0:T(1,128)S(1)} %get-tuple-element.146, f32[1,32768]{1,0:T(1,128)S(1)} %get-tuple-element.147, f32[1,32768]{1,0:T(1,128)S(1)} %get-tuple-element.148, f32[4,128]{1,0:T(4,128)S(1)} %get-tuple-element.157, ...), kind=kOutput, calls=%fused_computation.4.clone.1 | convolution fusion | flops 205915136 | bytes 659457 | tf_op jit(solution)/shard_map/while/body/eval_jaxpr/dot_general | solution.py:71
  323.6 8.1 %fusion.154 = f32[4,128]{1,0:T(4,128)S(1)} fusion(s32[32768]{0:T(1024)S(1)} %bitcast.48, f32[1,32768]{1,0:T(1,128)S(1)} %get-tuple-element.145, f32[1,32768]{1,0:T(1,128)S(1)} %get-tuple-element.146, f32[1,32768]{1,0:T(1,128)S(1)} %get-tuple-element.147, f32[1,32768]{1,0:T(1,128)S(1)} %get-tuple-element.148, f32[4,128]{1,0:T(4,128)S(1)} %get-tuple-element.157, ...), kind=kOutput, calls=%fused_computation.4.clone.1 | convolution fusion | flops 205915136 | bytes 659457 | tf_op jit(solution)/shard_map/while/body/eval_jaxpr/dot_general | solution.py:71
  334.5 8.1 %fusion.154 = f32[4,128]{1,0:T(4,128)S(1)} fusion(s32[32768]{0:T(1024)S(1)} %bitcast.48, f32[1,32768]{1,0:T(1,128)S(1)} %get-tuple-element.145, f32[1,32768]{1,0:T(1,128)S(1)} %get-tuple-element.146, f32[1,32768]{1,0:T(1,128)S(1)} %get-tuple-element.147, f32[1,32768]{1,0:T(1,128)S(1)} %get-tuple-element.148, f32[4,128]{1,0:T(4,128)S(1)} %get-tuple-element.157, ...), kind=kOutput, calls=%fused_computation.4.clone.1 | convolution fusion | flops 205915136 | bytes 659457 | tf_op jit(solution)/shard_map/while/body/eval_jaxpr/dot_general | solution.py:71
  342.6 41.4 %psum.23 = f32[4,128]{1,0:T(4,128)S(1)} all-reduce(f32[4,128]{1,0:T(4,128)S(1)} %get-tuple-element.34), channel_id=1, replica_groups=mesh['row'=4,'col'=8] {'row','col'}, use_global_device_ids=true, to_apply=%region_7.8 | all-reduce | flops 512 | bytes 4096 | tf_op jit(solution)/shard_map/psum | solution.py:83
  (43 shorter events, 31.7 us)
Async XLA Ops:
  70.9 27.2 %collective-permute-start = (f32[2,16,32,256]{3,2,1,0:T(8,128)S(1)}, f32[2,16,32,256]{3,2,1,0:T(8,128)S(1)}, u32[]{:S(2)}, u32[]{:S(2)}) collective-permute-start(f32[2,16,32,256]{3,2,1,0:T(8,128)S(1)} %get-tuple-element.75), channel_id=1, source_target_pairs={{0,8},{8,16},{16,24},{1,9},{9,17},{17,25},{2,10},{10,18},{18,26},{... | collective-permute-start | bytes 3145736 | tf_op jit(solution)/shard_map/ppermute | solution.py:17
  75.9 46.8 %collective-permute-start.1 = (f32[2,16,32,256]{3,2,1,0:T(8,128)S(1)}, f32[2,16,32,256]{3,2,1,0:T(8,128)S(1)}, u32[]{:S(2)}, u32[]{:S(2)}) collective-permute-start(f32[2,16,32,256]{3,2,1,0:T(8,128)S(1)} %get-tuple-element.76), channel_id=1, source_target_pairs={{8,0},{16,8},{24,16},{9,1},{17,9},{25,17},{10,2},{18,10},{26,18},{... | collective-permute-start | bytes 3145736 | tf_op jit(solution)/shard_map/ppermute | solution.py:18
  98.2 25.1 %copy-start.4 = (f32[2,16,32,256]{3,2,1,0:T(8,128)}, f32[2,16,32,256]{3,2,1,0:T(8,128)S(1)}, u32[]{:S(2)}) copy-start(f32[2,16,32,256]{3,2,1,0:T(8,128)S(1)} %collective-permute-done) | copy-start | bytes 3145732
  122.6 1.1 copy-start.5
  123.7 6.3 %copy-start = (s32[32,32,256]{2,1,0:T(8,128)S(1)}, s32[32,32,256]{2,1,0:T(8,128)}, u32[]{:S(2)}) copy-start(s32[32,32,256]{2,1,0:T(8,128)} %param.8) | copy-start | bytes 3145732
  123.7 6.3 %copy-start.2 = (f32[32,32,256]{2,1,0:T(8,128)S(1)}, f32[32,32,256]{2,1,0:T(8,128)}, u32[]{:S(2)}) copy-start(f32[32,32,256]{2,1,0:T(8,128)} %param.7) | copy-start | bytes 3145732
  123.7 6.3 %copy-start.3 = (f32[32,32,256]{2,1,0:T(8,128)S(1)}, f32[32,32,256]{2,1,0:T(8,128)}, u32[]{:S(2)}) copy-start(f32[32,32,256]{2,1,0:T(8,128)} %param.6) | copy-start | bytes 3145732
  126.1 58.9 %collective-permute-start.2 = (f32[2,64,16,256]{3,2,1,0:T(8,128)}, f32[2,64,16,256]{3,2,1,0:T(8,128)}, u32[]{:S(2)}, u32[]{:S(2)}) collective-permute-start(f32[2,64,16,256]{3,2,1,0:T(8,128)} %get-tuple-element.73), channel_id=1, source_target_pairs={{0,1},{1,2},{2,3},{3,4},{4,5},{5,6},{6,7},{8,9},{9,10},{10,11},{11... | collective-permute-start | bytes 6291464 | tf_op jit(solution)/shard_map/ppermute | solution.py:17
  128.7 56.3 %collective-permute-start.3 = (f32[2,64,16,256]{3,2,1,0:T(8,128)}, f32[2,64,16,256]{3,2,1,0:T(8,128)}, u32[]{:S(2)}, u32[]{:S(2)}) collective-permute-start(f32[2,64,16,256]{3,2,1,0:T(8,128)} %get-tuple-element.74), channel_id=1, source_target_pairs={{1,0},{2,1},{3,2},{4,3},{5,4},{6,5},{7,6},{9,8},{10,9},{11,10},{12... | collective-permute-start | bytes 6291464 | tf_op jit(solution)/shard_map/ppermute | solution.py:18
  254.0 1.0 copy-start.1
where the time goes:
time: 387 us; the launch traced here: 385 us
  other arithmetic  153 us (40%)
  blocking collectives  88 us (23%)
  matrix products  64.8 us (17%)
  waiting for transfers between devices  45.5 us (12%)
  local copies, waits for them, and re-layouts  20.9 us (5%)
  starting transfers between devices  10.1 us (3%)
    add x3, other arithmetic, valid_taps(): total = total + taps[j] * lax.slice_in_dim(padded, j, j + count, axis=axis)  130 us
    dot_general x8, matrix products, accumulate(): lax.dot_general(powers, onehot, (((1,), (1,)), ((), ())), precision=lax.P...  64.8 us
    psum x1, blocking collectives, local(): lax.psum((jnp.sum(cover * galaxy), jnp.sum(cover * randoms)), ('row', 'co...  46.6 us
    psum x1, blocking collectives, local(): whole_sums = lax.psum(local_sums, ('row', 'col'))  41.4 us
    ppermute x2, waiting for transfers between devices, extended_2(): after = lax.ppermute(first, axis, down)  24.4 us
    ppermute x2, waiting for transfers between devices, extended_2(): before = lax.ppermute(last, axis, up)  21 us
    mul x8, other arithmetic, accumulate(): mvals * cvals * cvals * cvals  12 us
    dynamic_slice x8, local copies, waits for them, and re-layouts, local(): lax.scan(accumulate, jnp.zeros((4, NPATCH), jnp.float32), (flat_c, flat_m...  10.6 us
  transfers between devices with their start and end apart: 4, of which 2 were waited for; matrix products, arithmetic and copies ran while one was open for 2% of the time, Pallas kernels for 0%

commit v1 on v0

--- a/solution.py
+++ b/solution.py
@@ -42,7 +42,8 @@
     widths = ((0, 0), (0, 0), (0, 0), (radius, radius))
     zsmooth = valid_taps(jnp.pad(fields, widths), taps, radius, 3)
     cover = coverage.astype(jnp.float32)
-    totals = lax.psum((jnp.sum(cover * galaxy), jnp.sum(cover * randoms)), ("row", "col"))
+    inner = lax.psum((jnp.sum(cover * galaxy), jnp.sum(cover * randoms)), "col")
+    totals = lax.psum(inner, "row")
     extended = extended_2(zsmooth, (("row", 1), ("col", 2)), radius)
     xsmooth = valid_taps(extended, taps, radius, 1)
     smoothed = valid_taps(xsmooth, taps, radius, 2)

time: 387 us -> 379 us (0.979)
  blocking collectives: 88 us -> 81.9 us
    psum x1 -> x2, blocking collectives: 46.6 us -> 43.8 us  [the longest x1 34 us: local(): inner = lax.psum((jnp.sum(cover * galaxy), jnp.sum(cover * randoms)), 'col')]
where the time goes in v1:
time: 379 us; the launch traced here: 377 us
  other arithmetic  152 us (40%)
  blocking collectives  81.9 us (22%)
  matrix products  64.8 us (17%)
  waiting for transfers between devices  45.5 us (12%)
  local copies, waits for them, and re-layouts  20.9 us (6%)
  starting transfers between devices  10.1 us (3%)
    add x3, other arithmetic, valid_taps(): total = total + taps[j] * lax.slice_in_dim(padded, j, j + count, axis=axis)  129 us
    dot_general x8, matrix products, accumulate(): lax.dot_general(powers, onehot, (((1,), (1,)), ((), ())), precision=lax.P...  64.8 us
    psum x1, blocking collectives, local(): whole_sums = lax.psum(local_sums, ('row', 'col'))  38.1 us
    psum x1, blocking collectives, local(): inner = lax.psum((jnp.sum(cover * galaxy), jnp.sum(cover * randoms)), 'col')  34 us
    ppermute x2, waiting for transfers between devices, extended_2(): after = lax.ppermute(first, axis, down)  24.4 us
    ppermute x2, waiting for transfers between devices, extended_2(): before = lax.ppermute(last, axis, up)  21 us
    mul x8, other arithmetic, accumulate(): mvals * cvals * cvals * cvals  12 us
    dynamic_slice x8, local copies, waits for them, and re-layouts, local(): lax.scan(accumulate, jnp.zeros((4, NPATCH), jnp.float32), (flat_c, flat_m...  10.6 us
  transfers between devices with their start and end apart: 4, of which 2 were waited for; matrix products, arithmetic and copies ran while one was open for 2% of the time, Pallas kernels for 0%

profile of v1, /device:TPU:0, one launch (start us, length us, event | category | flops | bytes accessed | tf_op | source)
XLA Modules:
  0.0 377.4 jit_solution(1434159690589398422)
XLA Ops:
  3.4 3.1 pad_maximum_fusion.2
  6.5 63.3 %fusion.99 = f32[2,32,32,256]{3,2,1,0:T(8,128)S(1)} fusion(f32[2,32,32,256]{3,2,1,0:T(8,128)} %pad_maximum_fusion.2, f32[]{:T(128)} %bitcast.34, f32[]{:T(128)} %bitcast.33, f32[]{:T(128)} %bitcast.32, f32[]{:T(128)} %bitcast.31, f32[]{:T(128)} %bitcast.30, f32[]{:T(128)} %bitcast.29, f32[]{:T(128)} %bitcast.28, f32[]{:T(128)} %bitcast.27, f32[]{:T(128)} %bitcast.26, ...), kind=kLoop, calls=%fused_computation.171 | loop fusion | flops 34078720 | bytes 4194436 | tf_op jit(solution)/shard_map/add | solution.py:34
  70.1 4.9 %collective-permute-start = (f32[2,16,32,256]{3,2,1,0:T(8,128)S(1)}, f32[2,16,32,256]{3,2,1,0:T(8,128)S(1)}, u32[]{:S(2)}, u32[]{:S(2)}) collective-permute-start(f32[2,16,32,256]{3,2,1,0:T(8,128)S(1)} %get-tuple-element.77), channel_id=1, source_target_pairs={{0,8},{8,16},{16,24},{1,9},{9,17},{17,25},{2,10},{10,18},{18,26},{... | collective-permute-start | bytes 3145736 | tf_op jit(solution)/shard_map/ppermute | solution.py:17
  76.3 21.0 %collective-permute-done = f32[2,16,32,256]{3,2,1,0:T(8,128)S(1)} collective-permute-done((f32[2,16,32,256]{3,2,1,0:T(8,128)S(1)}, f32[2,16,32,256]{3,2,1,0:T(8,128)S(1)}, u32[]{:S(2)}, u32[]{:S(2)}) %collective-permute-start) | collective-permute-done | bytes 1048608 | tf_op jit(solution)/shard_map/ppermute | solution.py:17
  97.3 24.4 %collective-permute-done.1 = f32[2,16,32,256]{3,2,1,0:T(8,128)S(1)} collective-permute-done((f32[2,16,32,256]{3,2,1,0:T(8,128)S(1)}, f32[2,16,32,256]{3,2,1,0:T(8,128)S(1)}, u32[]{:S(2)}, u32[]{:S(2)}) %collective-permute-start.1) | collective-permute-done | bytes 1048608 | tf_op jit(solution)/shard_map/ppermute | solution.py:18
  122.8 2.4 fusion.147
  125.2 2.6 collective-permute-start.2
  130.2 34.0 %all-reduce.1 = (f32[]{:T(128)}, f32[]{:T(128)}) all-reduce(f32[]{:T(128)} %get-tuple-element.56, f32[]{:T(128)} %get-tuple-element.55), channel_id=1, replica_groups=mesh['row'=4,'col'=8] {'col'}, use_global_device_ids=true, to_apply=%region_1.2 | all-reduce | flops 2 | bytes 16 | tf_op jit(solution)/shard_map/psum | solution.py:45
  164.3 9.8 %all-reduce.2 = (f32[]{:T(128)}, f32[]{:T(128)}) all-reduce(f32[]{:T(128)} %get-tuple-element.67, f32[]{:T(128)} %get-tuple-element.68), channel_id=1, replica_groups=mesh['row'=4,'col'=8] {'row'}, use_global_device_ids=true, to_apply=%region_2.3 | all-reduce | flops 2 | bytes 16 | tf_op jit(solution)/shard_map/psum | solution.py:46
  175.1 2.5 reshape.25
  177.5 2.4 reshape.27
  181.2 3.3 pad_maximum_fusion
  184.4 36.4 %fusion.13 = f32[2,32,64,256]{3,2,1,0:T(8,128)S(1)} fusion(f32[2,64,64,256]{3,2,1,0:T(8,128)S(1)} %pad_maximum_fusion, f32[]{:T(128)} %bitcast.34, f32[]{:T(128)} %bitcast.33, f32[]{:T(128)} %bitcast.32, f32[]{:T(128)} %bitcast.31, f32[]{:T(128)} %bitcast.30, f32[]{:T(128)} %bitcast.29, f32[]{:T(128)} %bitcast.28, f32[]{:T(128)} %bitcast.27, f32[]{:T(128)} %bitcast.26, ...), kind=kLoop, calls=%fused_computation.52 | loop fusion | flops 68157440 | bytes 142606464 | tf_op jit(solution)/shard_map/add | solution.py:34
  220.8 28.9 %fusion.109 = f32[2,32,32,256]{3,2,1,0:T(8,128)S(1)} fusion(f32[2,32,64,256]{3,2,1,0:T(8,128)S(1)} %fusion.13, f32[]{:T(128)} %bitcast.34, f32[]{:T(128)} %bitcast.33, f32[]{:T(128)} %bitcast.32, f32[]{:T(128)} %bitcast.31, f32[]{:T(128)} %bitcast.30, f32[]{:T(128)} %bitcast.29, f32[]{:T(128)} %bitcast.28, f32[]{:T(128)} %bitcast.27, f32[]{:T(128)} %bitcast.26, ...), kind=kLoop, calls=%fused_computation.182 | loop fusion | flops 34078720 | bytes 71303296 | tf_op jit(solution)/shard_map/add | solution.py:34
  251.1 87.6 %while.11 = (s32[]{:T(128)}, f32[4,128]{1,0:T(4,128)S(1)}, f32[8,32768]{1,0:T(8,128)}, f32[8,32768]{1,0:T(8,128)S(1)}, s32[8,32768]{1,0:T(8,128)}, /*index=5*/s32[]{:T(128)}, s32[]{:T(128)}) while((s32[]{:T(128)}, f32[4,128]{1,0:T(4,128)S(1)}, f32[8,32768]{1,0:T(8,128)}, f32[8,32768]{1,0:T(8,128)S(1)}, s32[8,32768]{1,0:T(8,128)}, ...), condition=%wide.region_8.9_spmd.clone, body=%wide.region_7.8_spmd.clone.sunk | while | flops 206013440 | bytes 1708127 | solution.py:81
  253.9 8.1 %fusion.154 = f32[4,128]{1,0:T(4,128)S(1)} fusion(s32[32768]{0:T(1024)S(1)} %bitcast.48, f32[1,32768]{1,0:T(1,128)S(1)} %get-tuple-element.147, f32[1,32768]{1,0:T(1,128)S(1)} %get-tuple-element.148, f32[1,32768]{1,0:T(1,128)S(1)} %get-tuple-element.149, f32[1,32768]{1,0:T(1,128)S(1)} %get-tuple-element.150, f32[4,128]{1,0:T(4,128)S(1)} %get-tuple-element.159, ...), kind=kOutput, calls=%fused_computation.4.clone.1 | convolution fusion | flops 205915136 | bytes 659457 | tf_op jit(solution)/shard_map/while/body/eval_jaxpr/dot_general | solution.py:72
  264.8 8.1 %fusion.154 = f32[4,128]{1,0:T(4,128)S(1)} fusion(s32[32768]{0:T(1024)S(1)} %bitcast.48, f32[1,32768]{1,0:T(1,128)S(1)} %get-tuple-element.147, f32[1,32768]{1,0:T(1,128)S(1)} %get-tuple-element.148, f32[1,32768]{1,0:T(1,128)S(1)} %get-tuple-element.149, f32[1,32768]{1,0:T(1,128)S(1)} %get-tuple-element.150, f32[4,128]{1,0:T(4,128)S(1)} %get-tuple-element.159, ...), kind=kOutput, calls=%fused_computation.4.clone.1 | convolution fusion | flops 205915136 | bytes 659457 | tf_op jit(solution)/shard_map/while/body/eval_jaxpr/dot_general | solution.py:72
  275.8 8.1 %fusion.154 = f32[4,128]{1,0:T(4,128)S(1)} fusion(s32[32768]{0:T(1024)S(1)} %bitcast.48, f32[1,32768]{1,0:T(1,128)S(1)} %get-tuple-element.147, f32[1,32768]{1,0:T(1,128)S(1)} %get-tuple-element.148, f32[1,32768]{1,0:T(1,128)S(1)} %get-tuple-element.149, f32[1,32768]{1,0:T(1,128)S(1)} %get-tuple-element.150, f32[4,128]{1,0:T(4,128)S(1)} %get-tuple-element.159, ...), kind=kOutput, calls=%fused_computation.4.clone.1 | convolution fusion | flops 205915136 | bytes 659457 | tf_op jit(solution)/shard_map/while/body/eval_jaxpr/dot_general | solution.py:72
  286.8 8.1 %fusion.154 = f32[4,128]{1,0:T(4,128)S(1)} fusion(s32[32768]{0:T(1024)S(1)} %bitcast.48, f32[1,32768]{1,0:T(1,128)S(1)} %get-tuple-element.147, f32[1,32768]{1,0:T(1,128)S(1)} %get-tuple-element.148, f32[1,32768]{1,0:T(1,128)S(1)} %get-tuple-element.149, f32[1,32768]{1,0:T(1,128)S(1)} %get-tuple-element.150, f32[4,128]{1,0:T(4,128)S(1)} %get-tuple-element.159, ...), kind=kOutput, calls=%fused_computation.4.clone.1 | convolution fusion | flops 205915136 | bytes 659457 | tf_op jit(solution)/shard_map/while/body/eval_jaxpr/dot_general | solution.py:72
  297.7 8.1 %fusion.154 = f32[4,128]{1,0:T(4,128)S(1)} fusion(s32[32768]{0:T(1024)S(1)} %bitcast.48, f32[1,32768]{1,0:T(1,128)S(1)} %get-tuple-element.147, f32[1,32768]{1,0:T(1,128)S(1)} %get-tuple-element.148, f32[1,32768]{1,0:T(1,128)S(1)} %get-tuple-element.149, f32[1,32768]{1,0:T(1,128)S(1)} %get-tuple-element.150, f32[4,128]{1,0:T(4,128)S(1)} %get-tuple-element.159, ...), kind=kOutput, calls=%fused_computation.4.clone.1 | convolution fusion | flops 205915136 | bytes 659457 | tf_op jit(solution)/shard_map/while/body/eval_jaxpr/dot_general | solution.py:72
  308.7 8.1 %fusion.154 = f32[4,128]{1,0:T(4,128)S(1)} fusion(s32[32768]{0:T(1024)S(1)} %bitcast.48, f32[1,32768]{1,0:T(1,128)S(1)} %get-tuple-element.147, f32[1,32768]{1,0:T(1,128)S(1)} %get-tuple-element.148, f32[1,32768]{1,0:T(1,128)S(1)} %get-tuple-element.149, f32[1,32768]{1,0:T(1,128)S(1)} %get-tuple-element.150, f32[4,128]{1,0:T(4,128)S(1)} %get-tuple-element.159, ...), kind=kOutput, calls=%fused_computation.4.clone.1 | convolution fusion | flops 205915136 | bytes 659457 | tf_op jit(solution)/shard_map/while/body/eval_jaxpr/dot_general | solution.py:72
  319.6 8.1 %fusion.154 = f32[4,128]{1,0:T(4,128)S(1)} fusion(s32[32768]{0:T(1024)S(1)} %bitcast.48, f32[1,32768]{1,0:T(1,128)S(1)} %get-tuple-element.147, f32[1,32768]{1,0:T(1,128)S(1)} %get-tuple-element.148, f32[1,32768]{1,0:T(1,128)S(1)} %get-tuple-element.149, f32[1,32768]{1,0:T(1,128)S(1)} %get-tuple-element.150, f32[4,128]{1,0:T(4,128)S(1)} %get-tuple-element.159, ...), kind=kOutput, calls=%fused_computation.4.clone.1 | convolution fusion | flops 205915136 | bytes 659457 | tf_op jit(solution)/shard_map/while/body/eval_jaxpr/dot_general | solution.py:72
  330.6 8.1 %fusion.154 = f32[4,128]{1,0:T(4,128)S(1)} fusion(s32[32768]{0:T(1024)S(1)} %bitcast.48, f32[1,32768]{1,0:T(1,128)S(1)} %get-tuple-element.147, f32[1,32768]{1,0:T(1,128)S(1)} %get-tuple-element.148, f32[1,32768]{1,0:T(1,128)S(1)} %get-tuple-element.149, f32[1,32768]{1,0:T(1,128)S(1)} %get-tuple-element.150, f32[4,128]{1,0:T(4,128)S(1)} %get-tuple-element.159, ...), kind=kOutput, calls=%fused_computation.4.clone.1 | convolution fusion | flops 205915136 | bytes 659457 | tf_op jit(solution)/shard_map/while/body/eval_jaxpr/dot_general | solution.py:72
  338.7 38.1 %psum.39 = f32[4,128]{1,0:T(4,128)S(1)} all-reduce(f32[4,128]{1,0:T(4,128)S(1)} %get-tuple-element.34), channel_id=1, replica_groups=mesh['row'=4,'col'=8] {'row','col'}, use_global_device_ids=true, to_apply=%region_9.10 | all-reduce | flops 512 | bytes 4096 | tf_op jit(solution)/shard_map/psum | solution.py:84
  (44 shorter events, 33.3 us)
Async XLA Ops:
  70.1 27.2 %collective-permute-start = (f32[2,16,32,256]{3,2,1,0:T(8,128)S(1)}, f32[2,16,32,256]{3,2,1,0:T(8,128)S(1)}, u32[]{:S(2)}, u32[]{:S(2)}) collective-permute-start(f32[2,16,32,256]{3,2,1,0:T(8,128)S(1)} %get-tuple-element.77), channel_id=1, source_target_pairs={{0,8},{8,16},{16,24},{1,9},{9,17},{17,25},{2,10},{10,18},{18,26},{... | collective-permute-start | bytes 3145736 | tf_op jit(solution)/shard_map/ppermute | solution.py:17
  75.0 46.8 %collective-permute-start.1 = (f32[2,16,32,256]{3,2,1,0:T(8,128)S(1)}, f32[2,16,32,256]{3,2,1,0:T(8,128)S(1)}, u32[]{:S(2)}, u32[]{:S(2)}) collective-permute-start(f32[2,16,32,256]{3,2,1,0:T(8,128)S(1)} %get-tuple-element.78), channel_id=1, source_target_pairs={{8,0},{16,8},{24,16},{9,1},{17,9},{25,17},{10,2},{18,10},{26,18},{... | collective-permute-start | bytes 3145736 | tf_op jit(solution)/shard_map/ppermute | solution.py:18
  97.3 25.1 %copy-start.4 = (f32[2,16,32,256]{3,2,1,0:T(8,128)}, f32[2,16,32,256]{3,2,1,0:T(8,128)S(1)}, u32[]{:S(2)}) copy-start(f32[2,16,32,256]{3,2,1,0:T(8,128)S(1)} %collective-permute-done) | copy-start | bytes 3145732
  121.7 1.1 copy-start.5
  122.8 6.3 %copy-start = (s32[32,32,256]{2,1,0:T(8,128)S(1)}, s32[32,32,256]{2,1,0:T(8,128)}, u32[]{:S(2)}) copy-start(s32[32,32,256]{2,1,0:T(8,128)} %param.8) | copy-start | bytes 3145732
  122.8 6.3 %copy-start.2 = (f32[32,32,256]{2,1,0:T(8,128)S(1)}, f32[32,32,256]{2,1,0:T(8,128)}, u32[]{:S(2)}) copy-start(f32[32,32,256]{2,1,0:T(8,128)} %param.7) | copy-start | bytes 3145732
  122.8 6.3 %copy-start.3 = (f32[32,32,256]{2,1,0:T(8,128)S(1)}, f32[32,32,256]{2,1,0:T(8,128)}, u32[]{:S(2)}) copy-start(f32[32,32,256]{2,1,0:T(8,128)} %param.6) | copy-start | bytes 3145732
  125.2 55.9 %collective-permute-start.2 = (f32[2,64,16,256]{3,2,1,0:T(8,128)}, f32[2,64,16,256]{3,2,1,0:T(8,128)}, u32[]{:S(2)}, u32[]{:S(2)}) collective-permute-start(f32[2,64,16,256]{3,2,1,0:T(8,128)} %get-tuple-element.75), channel_id=1, source_target_pairs={{0,1},{1,2},{2,3},{3,4},{4,5},{5,6},{6,7},{8,9},{9,10},{10,11},{11... | collective-permute-start | bytes 6291464 | tf_op jit(solution)/shard_map/ppermute | solution.py:17
  127.8 53.3 %collective-permute-start.3 = (f32[2,64,16,256]{3,2,1,0:T(8,128)}, f32[2,64,16,256]{3,2,1,0:T(8,128)}, u32[]{:S(2)}, u32[]{:S(2)}) collective-permute-start(f32[2,64,16,256]{3,2,1,0:T(8,128)} %get-tuple-element.76), channel_id=1, source_target_pairs={{1,0},{2,1},{3,2},{4,3},{5,4},{6,5},{7,6},{9,8},{10,9},{11,10},{12... | collective-permute-start | bytes 6291464 | tf_op jit(solution)/shard_map/ppermute | solution.py:18
  250.1 1.0 copy-start.1
